TPU v7x, 256 devices: a whole 4x4x8 slice. The times are simulated.
256 devices in a mesh: rows: 32 (over y, x, core), lists: 8 (over z).
Axes of the slice: x: 4, y: 4, z: 8, core: 2. Of those that a mesh axis runs over, the one named last changes fastest.
Arguments:
- samples: bfloat16 [32768, 256], P('rows'), may hold values from -100 to 100
- centers: bfloat16 [32768, 256], P('lists'), may hold values from -4 to 4
Outputs:
- assignment: bfloat16 [32768, 32768], P('rows', 'lists')
- new_centers: float32 [32768, 256], P(('lists', 'rows'))
All inputs are finite; a program needn't handle non-finite values.
Results may differ from a plain program's by a relative error of at most 0.0054.
Values may be sent and summed in bfloat16 or wider, within the bound.
A program may use at most 128 MiB of HBM per device.

v0:
```python
import jax
import jax.numpy as jnp
from jax import lax
from jax.sharding import PartitionSpec as P

ITERS = 3


SOFTMAX_TEMP_VALUE = 0.03


def unit_norm(value_entries):
    wide = value_entries.astype(jnp.float32)
    return (wide / jnp.sqrt(jnp.sum(wide * wide, 1, keepdims=True) + 1e-06)).astype(jnp.bfloat16)


def body(samples, centers):
    row_count = samples.shape[0]
    list_count = centers.shape[0]
    width = samples.shape[1]
    row_devices = lax.axis_size("rows")
    total_rows = row_count * row_devices
    total_lists = list_count * lax.axis_size("lists")
    unit_rows = unit_norm(samples)
    unit_centers = unit_norm(centers)
    affinity_scores = lax.dot_general(
        unit_rows, unit_centers, (((1,), (1,)), ((), ())), preferred_element_type=jnp.float32
    )
    kmeans_kernel = jnp.exp(affinity_scores / SOFTMAX_TEMP_VALUE)
    row_scaling_factor = jnp.ones((row_count,), jnp.float32)
    list_scale = jnp.ones((list_count,), jnp.float32)
    for step in range(ITERS):
        column_total = lax.psum(jnp.sum(row_scaling_factor[:, None] * kmeans_kernel, 0), "rows")
        list_scale = 1.0 / (total_lists * column_total)
        row_total = lax.psum(jnp.sum(kmeans_kernel * list_scale[None, :], 1), "lists")
        row_scaling_factor = 1.0 / (total_rows * row_total)
    assignment = (
        total_rows * row_scaling_factor[:, None] * kmeans_kernel * list_scale[None, :]
    ).astype(jnp.bfloat16)
    piece = list_count // row_devices
    list_mass = lax.psum(jnp.sum(assignment.astype(jnp.float32), 0), "rows")
    own_mass = lax.dynamic_slice_in_dim(list_mass, lax.axis_index("rows") * piece, piece, 0)
    weighted_sum = lax.psum_scatter(
        lax.dot_general(
            assignment, unit_rows, (((0,), (0,)), ((), ())), preferred_element_type=jnp.float32
        ),
        "rows",
        scatter_dimension=0,
        tiled=True,
    )
    new_centers = jnp.sqrt(jnp.float32(width)) * weighted_sum / own_mass[:, None]
    return (assignment, new_centers)


def solution(mesh):
    placed = (P("rows", None), P("lists", None))
    return jax.shard_map(
        body,
        mesh=mesh,
        in_specs=placed,
        out_specs=(P("rows", "lists"), P(("lists", "rows"), None)),
        check_vma=False,
    )
```

profile of v0, /device:TPU:1, one launch (start us, length us, event | category | flops | bytes accessed | tf_op | source)
XLA Modules:
  0.0 625.3 jit_solution(12506154509321110464)
XLA Ops:
  7.2 0.0 reduce-scatter.2.cloned.1.call-start
  7.2 1.3 fusion.4
  8.5 2.2 fusion
  10.7 8.8 %fusion.9 = (f32[4096]{0:T(1024)S(1)}, f32[1024,4096]{1,0:T(8,128)}) fusion(bf16[4096,256]{1,0:T(8,128)(2,1)} %param.3, f32[4096]{0:T(1024)S(1)} %add_sqrt_fusion, bf16[1024,256]{1,0:T(8,128)(2,1)} %param.2, f32[1024]{0:T(1024)S(1)} %add_sqrt_fusion.1), kind=kOutput, calls=%fused_computation.27 | convolution fusion | flops 2159800320 | bytes 19435520 | tf_op jit(solution)/shard_map/dot_general | solution.py:26
  19.6 124.2 %psum.49 = f32[4096]{0:T(1024)S(1)} all-reduce(f32[4096]{0:T(1024)S(1)} %get-tuple-element.4), channel_id=1, replica_groups=mesh['rows'=32,'lists'=8] {'rows'}, use_global_device_ids=true, to_apply=%region_3.0 | all-reduce | flops 4096 | bytes 32768 | tf_op jit(solution)/shard_map/psum | solution.py:33
  143.8 7.1 %multiply_reduce_fusion.4 = f32[1024]{0:T(1024)S(1)} fusion(f32[1024,4096]{1,0:T(8,128)} %get-tuple-element.5, f32[4096]{0:T(1024)S(1)} %multiply_divide_fusion.3), kind=kLoop, calls=%fused_computation.6 | loop fusion | flops 8387584 | bytes 16797696 | tf_op jit(solution)/shard_map/reduce_sum | solution.py:35
  150.8 16.3 %psum.50 = f32[1024]{0:T(1024)S(1)} all-reduce(f32[1024]{0:T(1024)S(1)} %multiply_reduce_fusion.4), channel_id=1, replica_groups=mesh['rows'=32,'lists'=8] {'lists'}, use_global_device_ids=true, to_apply=%region_5.0 | all-reduce | flops 1024 | bytes 8192 | tf_op jit(solution)/shard_map/psum | solution.py:35
  167.1 7.2 %multiply_reduce_fusion.3 = f32[4096]{0:T(1024)S(1)} fusion(f32[1024,4096]{1,0:T(8,128)} %get-tuple-element.5, f32[1024]{0:T(1024)S(1)} %multiply_divide_fusion.5), kind=kLoop, calls=%fused_computation.5 | loop fusion | flops 8384512 | bytes 16797696 | tf_op jit(solution)/shard_map/reduce_sum | solution.py:33
  174.3 127.5 %psum.51 = f32[4096]{0:T(1024)S(1)} all-reduce(f32[4096]{0:T(1024)S(1)} %multiply_reduce_fusion.3), channel_id=1, replica_groups=mesh['rows'=32,'lists'=8] {'rows'}, use_global_device_ids=true, to_apply=%region_7.0 | all-reduce | flops 4096 | bytes 32768 | tf_op jit(solution)/shard_map/psum | solution.py:33
  301.8 7.1 %multiply_reduce_fusion.2 = f32[1024]{0:T(1024)S(1)} fusion(f32[1024,4096]{1,0:T(8,128)} %get-tuple-element.5, f32[4096]{0:T(1024)S(1)} %multiply_divide_fusion.2), kind=kLoop, calls=%fused_computation.4 | loop fusion | flops 8387584 | bytes 16797696 | tf_op jit(solution)/shard_map/reduce_sum | solution.py:35
  308.9 10.7 %psum.52 = f32[1024]{0:T(1024)S(1)} all-reduce(f32[1024]{0:T(1024)S(1)} %multiply_reduce_fusion.2), channel_id=1, replica_groups=mesh['rows'=32,'lists'=8] {'lists'}, use_global_device_ids=true, to_apply=%region_9.0 | all-reduce | flops 1024 | bytes 8192 | tf_op jit(solution)/shard_map/psum | solution.py:35
  319.5 7.2 %multiply_reduce_fusion.1 = f32[4096]{0:T(1024)S(1)} fusion(f32[1024,4096]{1,0:T(8,128)} %get-tuple-element.5, f32[1024]{0:T(1024)S(1)} %multiply_divide_fusion.4), kind=kLoop, calls=%fused_computation.3 | loop fusion | flops 8384512 | bytes 16797696 | tf_op jit(solution)/shard_map/reduce_sum | solution.py:33
  326.7 127.3 %psum.53 = f32[4096]{0:T(1024)S(1)} all-reduce(f32[4096]{0:T(1024)S(1)} %multiply_reduce_fusion.1), channel_id=1, replica_groups=mesh['rows'=32,'lists'=8] {'rows'}, use_global_device_ids=true, to_apply=%region_11.0 | all-reduce | flops 4096 | bytes 32768 | tf_op jit(solution)/shard_map/psum | solution.py:33
  454.0 6.9 %multiply_reduce_fusion = f32[1024]{0:T(1024)S(1)} fusion(f32[1024,4096]{1,0:T(8,128)} %get-tuple-element.5, f32[4096]{0:T(1024)S(1)} %multiply_divide_fusion.1), kind=kLoop, calls=%fused_computation.2 | loop fusion | flops 8387584 | bytes 16797696 | tf_op jit(solution)/shard_map/reduce_sum | solution.py:35
  460.9 0.0 copy-start.1
  460.9 12.7 %psum.54 = f32[1024]{0:T(1024)S(1)} all-reduce(f32[1024]{0:T(1024)S(1)} %multiply_reduce_fusion), channel_id=1, replica_groups=mesh['rows'=32,'lists'=8] {'lists'}, use_global_device_ids=true, to_apply=%region_13.0 | all-reduce | flops 1024 | bytes 8192 | tf_op jit(solution)/shard_map/psum | solution.py:35
  473.6 7.3 %convert_reduce_fusion = (f32[4096]{0:T(1024)S(1)}, bf16[1024,4096]{1,0:T(8,128)(2,1)S(1)}) fusion(f32[4096]{0:T(1024)S(1)} %multiply_divide_fusion.1, f32[1024,4096]{1,0:T(8,128)} %get-tuple-element.5, f32[1024]{0:T(1024)S(1)} %divide_multiply_fusion), kind=kLoop, calls=%fused_computation | loop fusion | flops 20967424 | bytes 25202688 | tf_op jit(solution)/shard_map/reduce_sum | solution.py:41
  480.9 0.0 copy-start
  480.9 3.4 copy-done
  484.3 0.0 copy-done.1
  484.3 4.5 fusion.6
  488.8 0.0 reduce-scatter.2.cloned.1.call-update
  488.9 127.8 %psum.55 = f32[4096]{0:T(1024)S(1)} all-reduce(f32[4096]{0:T(1024)S(1)} %get-tuple-element.2), channel_id=1, replica_groups=mesh['rows'=32,'lists'=8] {'rows'}, use_global_device_ids=true, to_apply=%region_16.0 | all-reduce | flops 4096 | bytes 32768 | tf_op jit(solution)/shard_map/psum | solution.py:41
  616.7 0.1 dynamic_slice.3
  616.8 0.0 reduce-scatter.2.cloned.1.call-done
  616.8 1.6 multiply_divide_fusion
  (8 shorter events, 0.1 us)
Async XLA Ops:
  7.2 609.6 %reduce-scatter.2.cloned.1.call-start = ((), (), s32[]{:S(2)}) async-start(), calls=%async_computation.1 | async-start | bytes 4325376 | tf_op jit(solution)/shard_map/reduce_scatter | solution.py:43
  460.9 23.4 %copy-start.1 = (bf16[1024,256]{1,0:T(8,128)(2,1)S(1)}, bf16[1024,256]{1,0:T(8,128)(2,1)}, u32[]{:S(2)}) copy-start(bf16[1024,256]{1,0:T(8,128)(2,1)} %param.2) | copy-start | bytes 1572868
  480.9 3.4 copy-start
Sparse Core Ops, SparseCore 0:
  489.0 89.7 reduce-scatter.1
where the time goes:
time: 628 us; the launch traced here: 625 us
  blocking collectives  546 us (87%)
  other arithmetic  47.8 us (8%)
  between operations  14.1 us (2%)
  matrix products  13.4 us (2%)
    psum x3, blocking collectives, body(): lax.psum(jnp.sum(row_scaling_factor[:, None] * kmeans_kernel, 0), 'rows')  379 us
    psum x1, blocking collectives, body(): list_mass = lax.psum(jnp.sum(assignment.astype(jnp.float32), 0), 'rows')  128 us
    psum x3, blocking collectives, body(): lax.psum(jnp.sum(kmeans_kernel * list_scale[None, :], 1), 'lists')  39.6 us
    reduce_sum x3, other arithmetic, body(): jnp.sum(kmeans_kernel * list_scale[None, :], 1)  21.1 us
    reduce_sum x2, other arithmetic, body(): jnp.sum(row_scaling_factor[:, None] * kmeans_kernel, 0)  14.3 us
  transfers between devices with their start and end apart: 1, of which 0 were waited for; matrix products, arithmetic and copies ran while one was open for 0% of the time, Pallas kernels for 0%

commit v1 on v0

v1 whole, which is shorter than its diff:
```python
import functools

import jax
import jax.numpy as jnp
from jax import lax
from jax.experimental import pallas as pl
from jax.experimental.pallas import tpu as pltpu
from jax.sharding import PartitionSpec as P

ITERS = 3
SOFTMAX_TEMP_VALUE = 0.03
EXP2_SCALE = 1.0 / (SOFTMAX_TEMP_VALUE * 0.6931471805599453)
F32 = jnp.float32
BF16 = jnp.bfloat16
MESH = pl.DeviceIdType.MESH
NT = (((1,), (1,)), ((), ()))
LANES = 128


def unit_norm(block):
    wide = block.astype(F32)
    scale = 1.0 / jnp.sqrt(jnp.sum(wide * wide, 1, keepdims=True) + 1e-06)
    return (wide * scale).astype(BF16)


def affinity(left, right):
    scores = lax.dot_general(left, right, NT, preferred_element_type=F32)
    return jnp.exp2(scores * EXP2_SCALE)


def hops(step, size):
    return min(step, size - step)


def kernel(
    ny, nx, nz, total_rows, total_lists,
    samples, centers, out, new_centers,
    uall, cn, km, ko, kt, ut, stage, lhs, lhs_w, rcol,
    msg_c, msg_r, slots_c, slots_r, part_msg, part_in, list_in, list_own,
    w_out, w_in, row_out,
    ssem_c, rsem_c, ssem_r, rsem_r, sib_s, sib_r, ssem_w, rsem_w, out_sem,
):
    rows = samples.shape[0]
    half = centers.shape[0] // 2
    chip_rows = 2 * rows
    width = samples.shape[1]
    chips = ny * nx

    place = lax.axis_index("rows")
    z = lax.axis_index("lists")
    y = place // (2 * nx)
    x = (place // 2) % nx
    c = place % 2
    other = 1 - c

    def at(dy, dx, dc, dz):
        return (
            (((y + dy) % ny) * nx + (x + dx) % nx) * 2 + (c + dc) % 2,
            (z + dz) % nz,
        )

    sibling = at(0, 0, 1, 0)
    xy = [(dy, dx) for dy in range(ny) for dx in range(nx) if (dy, dx) != (0, 0)]
    xy.sort(key=lambda o: -(hops(o[0], ny) + hops(o[1], nx)))
    zc = [(dz, dc) for dz in range(nz) for dc in range(2) if (dz, dc) != (0, 0)]
    zc.sort(key=lambda o: -hops(o[0], nz))

    barrier = pltpu.get_barrier_semaphore()
    for dy, dx in xy:
        pl.semaphore_signal(barrier, inc=1, device_id=at(dy, dx, 0, 0), device_id_type=MESH)
    for dz, dc in zc:
        pl.semaphore_signal(barrier, inc=1, device_id=at(0, 0, dc, dz), device_id_type=MESH)

    own_rows = pl.ds(pl.multiple_of(c * rows, rows), rows)
    sib_rows = pl.ds(pl.multiple_of(other * rows, rows), rows)

    def norm_centers(which, parity):
        def step(j, _):
            src = pl.ds(pl.multiple_of((2 * j + parity) * LANES, LANES), LANES)
            dst = pl.ds(pl.multiple_of(j * LANES, LANES), LANES)
            cn[which, dst, :] = unit_norm(centers[src, :])
            return 0

        lax.fori_loop(0, half // LANES, step, 0)

    def to_rows(dst, vec):
        for i in range(dst.shape[0]):
            dst[i : i + 1, :] = vec[:, i * LANES : (i + 1) * LANES]

    def split_lhs(compact):
        high = compact.astype(BF16).astype(F32)
        low = compact - high
        for i in range(compact.shape[0]):
            lhs[0:1, i * LANES : (i + 1) * LANES] = high[i : i + 1, :]
            lhs[1:2, i * LANES : (i + 1) * LANES] = low[i : i + 1, :]

    def matvec(count, mat):
        got = jnp.dot(lhs[:, :count].astype(BF16), mat[...], preferred_element_type=F32)
        return got[0:1, :] + got[1:2, :]

    def exchange_start(msg, slots, ssem, rsem, targets):
        for slot, target in targets:
            pltpu.make_async_remote_copy(
                src_ref=msg, dst_ref=slots.at[slot], send_sem=ssem, recv_sem=rsem,
                device_id=target, device_id_type=MESH,
            ).start()

    def exchange_sum(msg, slots, rsem, count):
        arrived = slots.at[pl.ds(1, count - 1)]
        pltpu.make_async_copy(arrived, arrived, rsem).wait()
        total = msg[...]
        for i in range(1, count):
            total = total + slots[i]
        return total

    def sent(slots, ssem, count):
        gone = slots.at[pl.ds(1, count - 1)]
        pltpu.make_async_copy(gone, gone, ssem).wait()

    targets_c = [(dy * nx + dx, at(dy, dx, 0, 0)) for dy, dx in xy]
    targets_r = [(dz * 2 + dc, at(0, 0, dc, dz)) for dz, dc in zc]

    lhs[...] = jnp.zeros_like(lhs)
    uall[own_rows, :] = unit_norm(samples[...])
    norm_centers(1, other)
    block = affinity(uall[own_rows, :], cn[1])
    ko[...] = block.astype(BF16)
    to_rows(part_msg, jnp.sum(block, 0, keepdims=True))
    pl.semaphore_wait(barrier, len(xy) + len(zc))
    send_part = pltpu.make_async_remote_copy(
        src_ref=part_msg, dst_ref=part_in, send_sem=sib_s.at[0], recv_sem=sib_r.at[0],
        device_id=sibling, device_id_type=MESH,
    )
    send_part.start()
    send_rows = pltpu.make_async_remote_copy(
        src_ref=uall.at[own_rows], dst_ref=uall.at[own_rows],
        send_sem=sib_s.at[1], recv_sem=sib_r.at[1],
        device_id=sibling, device_id_type=MESH,
    )
    send_rows.start()
    norm_centers(0, c)
    block = affinity(uall[own_rows, :], cn[0])
    km[own_rows, :] = block.astype(BF16)
    to_rows(msg_c.at[0], jnp.sum(block, 0, keepdims=True))
    send_part.wait()
    msg_c[0] = msg_c[0] + part_in[...]

    send_lists = None
    row_scale = None
    list_scale = None
    for it in range(ITERS):
        if it > 0:
            split_lhs(row_scale)
            to_rows(msg_c.at[it], matvec(chip_rows, km))
        exchange_start(msg_c.at[it], slots_c.at[it], ssem_c.at[it], rsem_c.at[it], targets_c)
        if it == 0:
            kt[:, own_rows] = affinity(cn[0], uall[own_rows, :]).astype(BF16)
            send_rows.wait()
            kt[:, sib_rows] = affinity(cn[0], uall[sib_rows, :]).astype(BF16)
        column_total = exchange_sum(msg_c.at[it], slots_c.at[it], rsem_c.at[it], chips)
        list_scale = 1.0 / (total_lists * column_total)
        if it == ITERS - 1:
            list_own[...] = list_scale
            send_lists = pltpu.make_async_remote_copy(
                src_ref=list_own, dst_ref=list_in, send_sem=sib_s.at[2], recv_sem=sib_r.at[2],
                device_id=sibling, device_id_type=MESH,
            )
            send_lists.start()
        split_lhs(list_scale)
        to_rows(msg_r.at[it], matvec(half, kt))
        exchange_start(msg_r.at[it], slots_r.at[it], ssem_r.at[it], rsem_r.at[it], targets_r)
        if it == 0:
            km[sib_rows, :] = affinity(uall[sib_rows, :], cn[0]).astype(BF16)
            ut[...] = uall[...].astype(F32).T
        row_total = exchange_sum(msg_r.at[it], slots_r.at[it], rsem_r.at[it], 2 * nz)
        row_scale = 1.0 / (total_rows * row_total)

    for i in range(chip_rows // LANES):
        lanes = pl.ds(i * LANES, LANES)
        one = row_scale[i : i + 1, :]
        lhs_w[0:width, lanes] = (ut[:, lanes] * one).astype(BF16)
        high = one.astype(BF16).astype(F32)
        index = lax.broadcasted_iota(jnp.int32, (16, LANES), 0)
        lhs_w[width : width + 16, lanes] = jnp.where(
            index == 0, high, jnp.where(index == 1, one - high, 0.0)
        ).astype(BF16)

    order = [(dy, dx) for dy, dx in xy] + [(0, 0)]
    for g in range(0, chips, 4):
        group = order[g : g + 4]
        blocks = []
        for dy, dx in group:
            dest = ((y + dy) % ny) * nx + (x + dx) % nx
            blocks.append(km[:, pl.ds(pl.multiple_of(dest * LANES, LANES), LANES)])
        got = jnp.dot(
            lhs_w[...], jnp.concatenate(blocks, 1), preferred_element_type=F32
        )
        for n, (dy, dx) in enumerate(group):
            slot = dy * nx + dx
            piece = got[:, n * LANES : (n + 1) * LANES]
            mass = piece[width : width + 1] + piece[width + 1 : width + 2]
            high = mass.astype(BF16).astype(F32)
            mid = (mass - high).astype(BF16).astype(F32)
            index = lax.broadcasted_iota(jnp.int32, (16, LANES), 0)
            tail = jnp.where(
                index == 0, high,
                jnp.where(index == 1, mid, jnp.where(index == 2, mass - high - mid, 0.0)),
            )
            dst = w_in if slot == 0 else w_out
            dst[slot, 0:width, :] = piece[0:width].astype(BF16)
            dst[slot, width : width + 16, :] = tail.astype(BF16)
            if slot != 0:
                pltpu.make_async_remote_copy(
                    src_ref=w_out.at[slot], dst_ref=w_in.at[slot],
                    send_sem=ssem_w, recv_sem=rsem_w,
                    device_id=at(dy, dx, 0, 0), device_id_type=MESH,
                ).start()

    row_out[...] = total_rows * row_scale
    first = c * (rows // LANES)
    for i in range(rows // LANES):
        line = row_out[pl.ds(first + i, 1), :]
        rcol[i * LANES : (i + 1) * LANES, :] = jnp.broadcast_to(line, (LANES, LANES)).T
    send_lists.wait()

    def assign(i, _):
        block_rows = pl.ds(pl.multiple_of(i * LANES, LANES), LANES)
        main_rows = pl.ds(pl.multiple_of(c * rows + i * LANES, LANES), LANES)

        def inner(q, _):
            at_rows = pl.ds(pl.multiple_of(i * LANES + q * 16, 16), 16)
            at_main = pl.ds(pl.multiple_of(c * rows + i * LANES + q * 16, 16), 16)
            scale = rcol[at_rows, :]
            for j in range(half // LANES):
                lanes = pl.ds(j * LANES, LANES)
                one = km[at_main, lanes].astype(F32) * scale * list_own[j : j + 1, :]
                two = ko[at_rows, lanes].astype(F32) * scale * list_in[j : j + 1, :]
                stage[at_rows, pl.ds(pl.multiple_of((2 * j + c) * LANES, LANES), LANES)] = (
                    one.astype(BF16)
                )
                stage[at_rows, pl.ds(pl.multiple_of((2 * j + other) * LANES, LANES), LANES)] = (
                    two.astype(BF16)
                )
            return 0

        lax.fori_loop(0, LANES // 16, inner, 0)
        pltpu.make_async_copy(stage.at[block_rows], out.at[block_rows], out_sem).start()
        return 0

    lax.fori_loop(0, rows // LANES, assign, 0)

    arrived = w_in.at[pl.ds(1, chips - 1)]
    pltpu.make_async_copy(arrived, arrived, rsem_w).wait()
    total = w_in[0].astype(F32)
    for i in range(1, chips):
        total = total + w_in[i].astype(F32)
    mass = total[width : width + 1] + total[width + 1 : width + 2] + total[width + 2 : width + 3]
    new_centers[...] = (jnp.sqrt(F32(width)) * total[0:width] / mass).T

    sent(w_in, ssem_w, chips)
    for it in range(ITERS):
        sent(slots_c.at[it], ssem_c.at[it], chips)
        sent(slots_r.at[it], ssem_r.at[it], 2 * nz)
    pltpu.make_async_copy(stage, out, out_sem).wait()


def solution(mesh):
    row_devices = mesh.shape["rows"]
    nz = mesh.shape["lists"]
    ny = nx = round((row_devices // 2) ** 0.5)

    def body(samples, centers):
        rows, width = samples.shape
        lists = centers.shape[0]
        half, chip_rows, chips = lists // 2, 2 * rows, ny * nx
        mc, mr = half // LANES, chip_rows // LANES
        dma = pltpu.SemaphoreType.DMA
        vmem = pl.BlockSpec(memory_space=pltpu.VMEM)
        return pl.pallas_call(
            functools.partial(
                kernel, ny, nx, nz, float(rows * row_devices), float(lists * nz)
            ),
            out_shape=(
                jax.ShapeDtypeStruct((rows, lists), BF16),
                jax.ShapeDtypeStruct((lists // row_devices, width), F32),
            ),
            in_specs=[vmem, vmem],
            out_specs=(pl.BlockSpec(memory_space=pl.ANY), vmem),
            scratch_shapes=[
                pltpu.VMEM((chip_rows, width), BF16),
                pltpu.VMEM((2, half, width), BF16),
                pltpu.VMEM((chip_rows, half), BF16),
                pltpu.VMEM((rows, half), BF16),
                pltpu.VMEM((half, chip_rows), BF16),
                pltpu.VMEM((width, chip_rows), F32),
                pltpu.VMEM((rows, lists), BF16),
                pltpu.VMEM((16, max(half, chip_rows)), F32),
                pltpu.VMEM((width + 16, chip_rows), BF16),
                pltpu.VMEM((rows, LANES), F32),
                pltpu.VMEM((ITERS, mc, LANES), F32),
                pltpu.VMEM((ITERS, mr, LANES), F32),
                pltpu.VMEM((ITERS, chips, mc, LANES), F32),
                pltpu.VMEM((ITERS, 2 * nz, mr, LANES), F32),
                pltpu.VMEM((mc, LANES), F32),
                pltpu.VMEM((mc, LANES), F32),
                pltpu.VMEM((mc, LANES), F32),
                pltpu.VMEM((mc, LANES), F32),
                pltpu.VMEM((chips, width + 16, LANES), BF16),
                pltpu.VMEM((chips, width + 16, LANES), BF16),
                pltpu.VMEM((mr, LANES), F32),
                dma((ITERS,)),
                dma((ITERS,)),
                dma((ITERS,)),
                dma((ITERS,)),
                dma((3,)),
                dma((3,)),
                dma,
                dma,
                dma,
            ],
            compiler_params=pltpu.CompilerParams(
                collective_id=0, has_side_effects=True, vmem_limit_bytes=60 * 2**20
            ),
        )(samples, centers)

    return jax.shard_map(
        body,
        mesh=mesh,
        in_specs=(P("rows", None), P("lists", None)),
        out_specs=(P("rows", "lists"), P(("lists", "rows"), None)),
        check_vma=False,
    )
```

time: 628 us -> 78 us (0.12)
  blocking collectives: 546 us -> 0 us
  Pallas kernels: 0 us -> 68.7 us
  other arithmetic: 47.8 us -> 0 us
  between operations: 14.1 us -> 0.65 us
  matrix products: 13.4 us -> 0 us
    psum x7 -> x0, blocking collectives: 546 us -> none  [the longest x3 379 us: body(): lax.psum(jnp.sum(row_scaling_factor[:, None] * kmeans_kernel, 0), 'rows')]
    pallas_call x0 -> x1, Pallas kernels: none -> 68.7 us  [body(): pl.pallas_call(functools.partial(kernel, ny, nx, nz, float(rows * row_dev...]
    reduce_sum x8 -> x0, other arithmetic: 46.1 us -> none  [the longest x3 21.1 us: body(): jnp.sum(kmeans_kernel * list_scale[None, :], 1)]
    dot_general x2 -> x0, matrix products: 13.4 us -> none  [the longest x1 8.84 us: body(): lax.dot_general(unit_rows, unit_centers, (((1,), (1,)), ((), ())), prefer...]
  transfers between devices with their start and end apart: 1 -> 0, of which waited for: 0 -> 0; matrix products, arithmetic and copies ran while one was open for 0% -> 0% of each run, Pallas kernels for 0% -> 0%
where the time goes in v1:
time: 78 us; the launch traced here: 77.9 us
  Pallas kernels  68.7 us (88%)
  local copies, waits for them, and re-layouts  8.58 us (11%)
    pallas_call x1, Pallas kernels, body(): pl.pallas_call(functools.partial(kernel, ny, nx, nz, float(rows * row_dev...  68.7 us
    unnamed x4, local copies, waits for them, and re-layouts  8.58 us

profile of v1, /device:TPU:1, one launch (start us, length us, event | category | flops | bytes accessed | tf_op | source)
XLA Modules:
  0.0 77.9 jit_solution(16029813457314268258)
XLA Ops:
  0.6 68.7 %shard_map.41 = (bf16[1024,4096]{1,0:T(8,128)(2,1)}, f32[128,256]{1,0:T(8,128)}) custom-call(bf16[1024,256]{1,0:T(8,128)(2,1)} %samples.1, bf16[4096,256]{1,0:T(8,128)(2,1)} %centers.1), custom_call_target="tpu_custom_call" | custom-call | tf_op jit(solution)/shard_map/pallas_call | solution.py:279
  69.3 0.0 copy-start
  69.3 7.9 %copy.6 = bf16[1024,4096]{1,0:T(8,128)(2,1)} copy(bf16[1024,4096]{1,0:T(8,128)(2,1)} %get-tuple-element.4) | data formatting | bytes 16777216
  77.2 0.0 copy-done
  77.2 0.7 copy.7
Async XLA Ops:
  69.3 7.9 %copy-start = (f32[128,256]{1,0:T(8,128)S(1)}, f32[128,256]{1,0:T(8,128)}, u32[]{:S(2)}) copy-start(f32[128,256]{1,0:T(8,128)} %get-tuple-element.5) | copy-start | bytes 393220

commit v2 on v1

v2 whole, which is shorter than its diff:
```python
import functools

import jax
import jax.numpy as jnp
from jax import lax
from jax.experimental import pallas as pl
from jax.experimental.pallas import tpu as pltpu
from jax.sharding import PartitionSpec as P

ITERS = 3
SOFTMAX_TEMP_VALUE = 0.03
EXP2_SCALE = 1.0 / (SOFTMAX_TEMP_VALUE * 0.6931471805599453)
F32 = jnp.float32
BF16 = jnp.bfloat16
MESH = pl.DeviceIdType.MESH
NT = (((1,), (1,)), ((), ()))
LANES = 128


def unit_norm(block):
    wide = block.astype(F32)
    scale = 1.0 / jnp.sqrt(jnp.sum(wide * wide, 1, keepdims=True) + 1e-06)
    return (wide * scale).astype(BF16)


def affinity(left, right):
    scores = lax.dot_general(left, right, NT, preferred_element_type=F32)
    return jnp.exp2(scores * EXP2_SCALE)


def hops(step, size):
    return min(step, size - step)


def mass_rows(mass):
    high = mass.astype(BF16).astype(F32)
    mid = (mass - high).astype(BF16).astype(F32)
    index = lax.broadcasted_iota(jnp.int32, (16, LANES), 0)
    return jnp.where(
        index == 0, high,
        jnp.where(index == 1, mid, jnp.where(index == 2, mass - high - mid, 0.0)),
    ).astype(BF16)


def mass_of(tail):
    return tail[0:1] + tail[1:2] + tail[2:3]


def kernel(
    ny, nx, nz, total_rows, total_lists,
    samples, centers, out, new_centers,
    xs, cs, uall, cn, km, ko, kt, ut, lhs_w, rcol, sums,
    own_c, msg_c, slots_c, own_r, msg_r, slots_r, part_msg, part_in, list_own, list_in,
    w_out, wa1, wb1, wa2_out, wb2_out, wa2, wb2,
    in_sem, ssem_c, rsem_c, ssem_r, rsem_r, sib_s, sib_r,
    ss_a1, rs_a1, ss_b1, rs_b1, ss_2, rs_2,
):
    rows, width = xs.shape
    half = cs.shape[1] * LANES
    chip_rows = 2 * rows
    chips = ny * nx
    front = width // 2 + 16

    place = lax.axis_index("rows")
    z = lax.axis_index("lists")
    y = place // (2 * nx)
    x = (place // 2) % nx
    c = place % 2
    other = 1 - c

    def at(dy, dx, dc, dz):
        return (
            (((y + dy) % ny) * nx + (x + dx) % nx) * 2 + (c + dc) % 2,
            (z + dz) % nz,
        )

    def remote(src, dst, ssem, rsem, target):
        return pltpu.make_async_remote_copy(
            src_ref=src, dst_ref=dst, send_sem=ssem, recv_sem=rsem,
            device_id=target, device_id_type=MESH,
        )

    def settle(ref, sem):
        pltpu.make_async_copy(ref, ref, sem).wait()

    sibling = at(0, 0, 1, 0)
    xy = [(dy, dx) for dy in range(ny) for dx in range(nx) if (dy, dx) != (0, 0)]
    xy.sort(key=lambda o: -(hops(o[0], ny) + hops(o[1], nx)))
    zc = [(dz, dc) for dz in range(nz) for dc in range(2) if (dz, dc) != (0, 0)]
    zc.sort(key=lambda o: -hops(o[0], nz))

    barrier = pltpu.get_barrier_semaphore()
    for dy, dx in xy:
        pl.semaphore_signal(barrier, inc=1, device_id=at(dy, dx, 0, 0), device_id_type=MESH)
    for dz, dc in zc:
        pl.semaphore_signal(barrier, inc=1, device_id=at(0, 0, dc, dz), device_id_type=MESH)

    loads = [
        pltpu.make_async_copy(samples, xs, in_sem.at[0]),
        pltpu.make_async_copy(centers.at[:, other], cs.at[1], in_sem.at[1]),
        pltpu.make_async_copy(centers.at[:, c], cs.at[0], in_sem.at[2]),
    ]
    for load in loads:
        load.start()

    own_rows = pl.ds(pl.multiple_of(c * rows, rows), rows)
    sib_rows = pl.ds(pl.multiple_of(other * rows, rows), rows)

    def to_rows(dst, vec):
        for i in range(dst.shape[0]):
            dst[i : i + 1, :] = vec[:, i * LANES : (i + 1) * LANES]

    def spread(compact):
        for i in range(compact.shape[0]):
            rcol[i * LANES : (i + 1) * LANES, :] = jnp.broadcast_to(
                compact[i : i + 1, :], (LANES, LANES)
            ).T

    def contract(compact, mat, dst):
        spread(compact)
        depth, count = mat.shape
        total = None
        for i in range(0, depth, LANES):
            scale = jnp.concatenate([rcol[i : i + LANES, :]] * (count // LANES), 1)
            term = mat[i : i + LANES, :].astype(F32) * scale
            term = jnp.sum(term.reshape(LANES // 8, 8, count), 0)
            total = term if total is None else total + term
        for i in range(count // LANES):
            dst[i : i + 1, :] = jnp.sum(total[:, i * LANES : (i + 1) * LANES], 0, keepdims=True)

    def exchange_start(own, msg, slots, ssem, rsem, targets):
        msg[...] = own[...].astype(BF16)
        for slot, target in targets:
            remote(msg, slots.at[slot], ssem, rsem, target).start()

    def exchange_sum(own, slots, rsem, count):
        settle(slots.at[pl.ds(1, count - 1)], rsem)
        total = own[...]
        for i in range(1, count):
            total = total + slots[i].astype(F32)
        return total

    targets_c = [(dy * nx + dx, at(dy, dx, 0, 0)) for dy, dx in xy]
    targets_r = [(dz * 2 + dc, at(0, 0, dc, dz)) for dz, dc in zc]

    loads[0].wait()
    uall[own_rows, :] = unit_norm(xs[...])
    loads[1].wait()
    cn[1] = unit_norm(cs[1].reshape(half, width))
    block = affinity(uall[own_rows, :], cn[1])
    ko[...] = block.astype(BF16)
    to_rows(part_msg, jnp.sum(block, 0, keepdims=True))
    pl.semaphore_wait(barrier, len(xy) + len(zc))
    send_part = remote(part_msg, part_in, sib_s.at[0], sib_r.at[0], sibling)
    send_part.start()
    send_rows = remote(
        uall.at[own_rows], uall.at[own_rows], sib_s.at[1], sib_r.at[1], sibling
    )
    send_rows.start()
    loads[2].wait()
    cn[0] = unit_norm(cs[0].reshape(half, width))
    block = affinity(uall[own_rows, :], cn[0])
    km[own_rows, :] = block.astype(BF16)
    to_rows(sums, jnp.sum(block, 0, keepdims=True))
    send_part.wait()
    own_c[0] = sums[...] + part_in[...]

    send_lists = None
    row_scale = None
    for it in range(ITERS):
        if it > 0:
            contract(row_scale, km, own_c.at[it])
        exchange_start(
            own_c.at[it], msg_c.at[it], slots_c.at[it], ssem_c.at[it], rsem_c.at[it], targets_c
        )
        if it == 0:
            kt[:, own_rows] = affinity(cn[0], uall[own_rows, :]).astype(BF16)
            send_rows.wait()
            kt[:, sib_rows] = affinity(cn[0], uall[sib_rows, :]).astype(BF16)
        column_total = exchange_sum(own_c.at[it], slots_c.at[it], rsem_c.at[it], chips)
        list_scale = 1.0 / (total_lists * column_total)
        if it == ITERS - 1:
            list_own[...] = list_scale
            send_lists = remote(list_own, list_in, sib_s.at[2], sib_r.at[2], sibling)
            send_lists.start()
        contract(list_scale, kt, own_r.at[it])
        exchange_start(
            own_r.at[it], msg_r.at[it], slots_r.at[it], ssem_r.at[it], rsem_r.at[it], targets_r
        )
        if it == 0:
            km[sib_rows, :] = affinity(uall[sib_rows, :], cn[0]).astype(BF16)
            ut[...] = uall[...].astype(F32).T
        row_total = exchange_sum(own_r.at[it], slots_r.at[it], rsem_r.at[it], 2 * nz)
        row_scale = 1.0 / (total_rows * row_total)

    index = lax.broadcasted_iota(jnp.int32, (16, LANES), 0)
    for i in range(chip_rows // LANES):
        lanes = pl.ds(i * LANES, LANES)
        one = row_scale[i : i + 1, :]
        lhs_w[0:width, lanes] = (ut[:, lanes] * one).astype(BF16)
        high = one.astype(BF16).astype(F32)
        lhs_w[width : width + 16, lanes] = jnp.where(
            index == 0, high, jnp.where(index == 1, one - high, 0.0)
        ).astype(BF16)

    def reach(o):
        a, b = hops(o[0], ny), hops(o[1], nx)
        return -(4 * max(a, b) + a + b)

    order = sorted(xy + [(0, 0)], key=reach)
    for g in range(0, chips, 4):
        group = order[g : g + 4]
        blocks = []
        for dy, dx in group:
            dest = ((y + dy) % ny) * nx + (x + dx) % nx
            blocks.append(km[:, pl.ds(pl.multiple_of(dest * LANES, LANES), LANES)])
        got = jnp.dot(
            lhs_w[...], jnp.concatenate(blocks, 1), preferred_element_type=F32
        )
        for n, (dy, dx) in enumerate(group):
            slot = dy * nx + dx
            piece = got[:, n * LANES : (n + 1) * LANES]
            mass = piece[width : width + 1] + piece[width + 1 : width + 2]
            first = wa1.at[dy, 0] if dx == 0 else w_out.at[slot, pl.ds(0, front)]
            second = wb1.at[dx, 0] if dy == 0 else w_out.at[slot, pl.ds(front, width // 2)]
            first[0 : width // 2, :] = piece[0 : width // 2].astype(BF16)
            first[width // 2 : front, :] = mass_rows(mass)
            second[...] = piece[width // 2 : width].astype(BF16)
            if dx != 0:
                remote(first, wa1.at[dy, dx], ss_a1.at[dy], rs_a1.at[dy], at(0, dx, 0, 0)).start()
            if dy != 0:
                remote(second, wb1.at[dx, dy], ss_b1.at[dx], rs_b1.at[dx], at(dy, 0, 0, 0)).start()

    final_rows = total_rows * row_scale
    spread(final_rows)
    send_lists.wait()

    def assign(start, stop):
        for parity in range(2):
            @pl.when(c == parity)
            def _():
                def step(i, _):
                    here = pl.ds(pl.multiple_of(i * 16, 16), 16)
                    there = pl.ds(pl.multiple_of(parity * rows + i * 16, 16), 16)
                    scale = rcol[there, :]
                    for j in range(half // LANES):
                        lanes = pl.ds(j * LANES, LANES)
                        one = km[there, lanes].astype(F32) * scale * list_own[j : j + 1, :]
                        two = ko[here, lanes].astype(F32) * scale * list_in[j : j + 1, :]
                        out[here, pl.ds((2 * j + parity) * LANES, LANES)] = one.astype(BF16)
                        out[here, pl.ds((2 * j + 1 - parity) * LANES, LANES)] = two.astype(BF16)
                    return 0

                lax.fori_loop(start, stop, step, 0)

    steps = rows // 16
    assign(0, steps // 2)

    def gather(slots, count):
        total = slots[0].astype(F32)
        for i in range(1, count):
            total = total + slots[i].astype(F32)
        return total

    def stage_a(dy):
        settle(wa1.at[dy, pl.ds(1, nx - 1)], rs_a1.at[dy])
        return gather(wa1.at[dy], nx)

    def stage_b(dx):
        settle(wb1.at[dx, pl.ds(1, ny - 1)], rs_b1.at[dx])
        return gather(wb1.at[dx], ny)

    for step in sorted(range(1, ny), key=lambda o: -hops(o, ny)):
        total = stage_a(step)
        wa2_out[step, 0 : width // 2, :] = total[0 : width // 2].astype(BF16)
        wa2_out[step, width // 2 : front, :] = mass_rows(mass_of(total[width // 2 : front]))
        remote(wa2_out.at[step], wa2.at[step], ss_2.at[0], rs_2.at[0], at(step, 0, 0, 0)).start()
        total = stage_b(step)
        wb2_out[step] = total.astype(BF16)
        remote(wb2_out.at[step], wb2.at[step], ss_2.at[1], rs_2.at[1], at(0, step, 0, 0)).start()

    assign(steps // 2, steps)

    first = stage_a(0)
    second = stage_b(0)
    settle(wa2.at[pl.ds(1, ny - 1)], rs_2.at[0])
    for i in range(1, ny):
        first = first + wa2[i].astype(F32)
    settle(wb2.at[pl.ds(1, nx - 1)], rs_2.at[1])
    for i in range(1, nx):
        second = second + wb2[i].astype(F32)
    scale = jnp.sqrt(F32(width)) / mass_of(first[width // 2 : front])
    new_centers[:, 0 : width // 2] = (first[0 : width // 2] * scale).T
    new_centers[:, width // 2 : width] = (second * scale).T

    for i in range(ny):
        settle(wa1.at[i, pl.ds(1, nx - 1)], ss_a1.at[i])
    for i in range(nx):
        settle(wb1.at[i, pl.ds(1, ny - 1)], ss_b1.at[i])
    settle(wa2.at[pl.ds(1, ny - 1)], ss_2.at[0])
    settle(wb2.at[pl.ds(1, nx - 1)], ss_2.at[1])
    for it in range(ITERS):
        settle(slots_c.at[it, pl.ds(1, chips - 1)], ssem_c.at[it])
        settle(slots_r.at[it, pl.ds(1, 2 * nz - 1)], ssem_r.at[it])


def write_out(assignment, new_centers, out, out_centers, sems):
    pieces = 8
    size = assignment.shape[0] // pieces
    copies = [
        pltpu.make_async_copy(
            assignment.at[pl.ds(i * size, size)], out.at[pl.ds(i * size, size)], sems.at[i]
        )
        for i in range(pieces)
    ]
    copies.append(pltpu.make_async_copy(new_centers, out_centers, sems.at[pieces]))
    for copy in copies:
        copy.start()
    for copy in copies:
        copy.wait()


def solution(mesh):
    row_devices = mesh.shape["rows"]
    nz = mesh.shape["lists"]
    ny = nx = round((row_devices // 2) ** 0.5)

    def body(samples, centers):
        rows, width = samples.shape
        lists = centers.shape[0]
        half, chip_rows, chips = lists // 2, 2 * rows, ny * nx
        mc, mr = half // LANES, chip_rows // LANES
        front = width // 2 + 16
        dma = pltpu.SemaphoreType.DMA
        vmem = pl.BlockSpec(memory_space=pltpu.VMEM)
        hbm = pl.BlockSpec(memory_space=pl.ANY)
        big = ((rows, lists), BF16)
        small = ((lists // row_devices, width), F32)
        assignment, new_centers = pl.pallas_call(
            functools.partial(
                kernel, ny, nx, nz, float(rows * row_devices), float(lists * nz)
            ),
            out_shape=(pltpu.VMEM(*big), pltpu.VMEM(*small)),
            in_specs=[hbm, hbm],
            out_specs=(vmem, vmem),
            scratch_shapes=[
                pltpu.VMEM((rows, width), BF16),
                pltpu.VMEM((2, half // LANES, LANES, width), BF16),
                pltpu.VMEM((chip_rows, width), BF16),
                pltpu.VMEM((2, half, width), BF16),
                pltpu.VMEM((chip_rows, half), BF16),
                pltpu.VMEM((rows, half), BF16),
                pltpu.VMEM((half, chip_rows), BF16),
                pltpu.VMEM((width, chip_rows), F32),
                pltpu.VMEM((width + 16, chip_rows), BF16),
                pltpu.VMEM((max(half, chip_rows), LANES), F32),
                pltpu.VMEM((mc, LANES), F32),
                pltpu.VMEM((ITERS, mc, LANES), F32),
                pltpu.VMEM((ITERS, mc, LANES), BF16),
                pltpu.VMEM((ITERS, chips, mc, LANES), BF16),
                pltpu.VMEM((ITERS, mr, LANES), F32),
                pltpu.VMEM((ITERS, mr, LANES), BF16),
                pltpu.VMEM((ITERS, 2 * nz, mr, LANES), BF16),
                pltpu.VMEM((mc, LANES), F32),
                pltpu.VMEM((mc, LANES), F32),
                pltpu.VMEM((mc, LANES), F32),
                pltpu.VMEM((mc, LANES), F32),
                pltpu.VMEM((chips, width + 16, LANES), BF16),
                pltpu.VMEM((ny, nx, front, LANES), BF16),
                pltpu.VMEM((nx, ny, width // 2, LANES), BF16),
                pltpu.VMEM((ny, front, LANES), BF16),
                pltpu.VMEM((nx, width // 2, LANES), BF16),
                pltpu.VMEM((ny, front, LANES), BF16),
                pltpu.VMEM((nx, width // 2, LANES), BF16),
                dma((3,)),
                dma((ITERS,)),
                dma((ITERS,)),
                dma((ITERS,)),
                dma((ITERS,)),
                dma((3,)),
                dma((3,)),
                dma((ny,)),
                dma((ny,)),
                dma((nx,)),
                dma((nx,)),
                dma((2,)),
                dma((2,)),
            ],
            compiler_params=pltpu.CompilerParams(
                collective_id=0, has_side_effects=True, vmem_limit_bytes=50 * 2**20
            ),
        )(samples, centers.reshape(half // LANES, 2, LANES, width))
        return tuple(
            pl.pallas_call(
                write_out,
                out_shape=(jax.ShapeDtypeStruct(*big), jax.ShapeDtypeStruct(*small)),
                in_specs=[vmem, vmem],
                out_specs=(hbm, hbm),
                scratch_shapes=[dma((9,))],
                compiler_params=pltpu.CompilerParams(vmem_limit_bytes=2**20),
            )(
                pltpu.with_memory_space_constraint(assignment, pltpu.VMEM),
                pltpu.with_memory_space_constraint(new_centers, pltpu.VMEM),
            )
        )

    return jax.shard_map(
        body,
        mesh=mesh,
        in_specs=(P("rows", None), P("lists", None)),
        out_specs=(P("rows", "lists"), P(("lists", "rows"), None)),
        check_vma=False,
    )
```

time: 78 us -> 66 us (0.85)
  local copies, waits for them, and re-layouts: 8.58 us -> 0 us
  Pallas kernels: 68.7 us -> 65.1 us
    unnamed x4 -> x0, local copies, waits for them, and re-layouts: 8.58 us -> none
    pallas_call x1, Pallas kernels: 68.7 us -> 61.8 us  [body(): pl.pallas_call(functools.partial(kernel, ny, nx, nz, float(rows * row_dev...]
    pallas_call x0 -> x1, Pallas kernels: none -> 3.38 us  [body(): pl.pallas_call(write_out, out_shape=(jax.ShapeDtypeStruct(*big), jax.Shap...]
where the time goes in v2:
time: 66 us; the launch traced here: 65.9 us
  Pallas kernels  65.1 us (99%)
  between operations  0.8 us (1%)
    pallas_call x1, Pallas kernels, body(): pl.pallas_call(functools.partial(kernel, ny, nx, nz, float(rows * row_dev...  61.8 us
    pallas_call x1, Pallas kernels, body(): pl.pallas_call(write_out, out_shape=(jax.ShapeDtypeStruct(*big), jax.Shap...  3.38 us

profile of v2, /device:TPU:1, one launch (start us, length us, event | category | flops | bytes accessed | tf_op | source)
XLA Modules:
  0.0 65.9 jit_solution(17111939407516339235)
XLA Ops:
  0.6 61.8 %shard_map.41 = (bf16[1024,4096]{1,0:T(8,128)(2,1)S(1)}, f32[128,256]{1,0:T(8,128)S(1)}) custom-call(bf16[1024,256]{1,0:T(8,128)(2,1)} %samples.1, bf16[16,2,128,256]{3,2,1,0:T(8,128)(2,1)} %bitcast.1), custom_call_target="tpu_custom_call" | custom-call | tf_op jit(solution)/shard_map/pallas_call | solution.py:339
  62.4 3.4 %shard_map.42 = (bf16[1024,4096]{1,0:T(8,128)(2,1)}, f32[128,256]{1,0:T(8,128)}) custom-call(bf16[1024,4096]{1,0:T(8,128)(2,1)S(1)} %get-tuple-element.4.assignment, f32[128,256]{1,0:T(8,128)S(1)} %get-tuple-element.5.new_centers), custom_call_target="tpu_custom_call" | custom-call | tf_op jit(solution)/shard_map/pallas_call | solution.py:394

commit v3 on v2

v3 whole, which is shorter than its diff:
```python
import functools

import jax
import jax.numpy as jnp
from jax import lax
from jax.experimental import pallas as pl
from jax.experimental.pallas import tpu as pltpu
from jax.sharding import PartitionSpec as P

ITERS = 3
SOFTMAX_TEMP_VALUE = 0.03
EXP2_SCALE = 1.0 / (SOFTMAX_TEMP_VALUE * 0.6931471805599453)
F32 = jnp.float32
BF16 = jnp.bfloat16
MESH = pl.DeviceIdType.MESH
NT = (((1,), (1,)), ((), ()))
LANES = 128


def unit_norm(block):
    wide = block.astype(F32)
    return (wide * lax.rsqrt(jnp.sum(wide * wide, 1, keepdims=True) + 1e-06)).astype(BF16)


def affinity(left, right):
    scores = lax.dot_general(left, right, NT, preferred_element_type=F32)
    return jnp.exp2(scores * EXP2_SCALE)


def hops(step, size):
    return min(step, size - step)


def kernel(
    ny, nx, nz, total_rows, total_lists,
    samples, centers, out, raw,
    xs, cs, uall, cn, km, ko, kt, ut, lhs_w, rcol, sums,
    msg_0, slots_0, own_c, msg_c, slots_c, own_r, msg_r, slots_r, list_own, list_in,
    mass_out, mass_in, w_out, wa1, wb1, wa2_out, wb2_out, wa2, wb2,
    in_sem, sem_0, ssem_c, rsem_c, ssem_r, rsem_r, sib_s, sib_r, sem_m,
    ss_a1, rs_a1, ss_b1, rs_b1, ss_2, rs_2,
):
    rows, width = xs.shape
    half = cs.shape[1] * LANES
    chip_rows = 2 * rows
    chips = ny * nx
    part = width // 2

    place = lax.axis_index("rows")
    z = lax.axis_index("lists")
    y = place // (2 * nx)
    x = (place // 2) % nx
    c = place % 2
    other = 1 - c

    def at(dy, dx, dc, dz):
        return (
            (((y + dy) % ny) * nx + (x + dx) % nx) * 2 + (c + dc) % 2,
            (z + dz) % nz,
        )

    def remote(src, dst, ssem, rsem, target):
        return pltpu.make_async_remote_copy(
            src_ref=src, dst_ref=dst, send_sem=ssem, recv_sem=rsem,
            device_id=target, device_id_type=MESH,
        )

    def settle(ref, sem):
        pltpu.make_async_copy(ref, ref, sem).wait()

    sibling = at(0, 0, 1, 0)
    xy = [(dy, dx) for dy in range(ny) for dx in range(nx) if (dy, dx) != (0, 0)]
    xy.sort(key=lambda o: -(hops(o[0], ny) + hops(o[1], nx)))
    zc = [(dz, dc) for dz in range(nz) for dc in range(2) if (dz, dc) != (0, 0)]
    zc.sort(key=lambda o: -hops(o[0], nz))
    xyc = [(dy, dx, dc) for dy, dx in xy for dc in range(2)] + [(0, 0, 1)]

    loads = [
        pltpu.make_async_copy(samples, xs, in_sem.at[0]),
        pltpu.make_async_copy(centers.at[:, other], cs.at[1], in_sem.at[1]),
        pltpu.make_async_copy(centers.at[:, c], cs.at[0], in_sem.at[2]),
    ]
    for load in loads:
        load.start()

    barrier = pltpu.get_barrier_semaphore()
    for dy, dx, dc in xyc:
        pl.semaphore_signal(barrier, inc=1, device_id=at(dy, dx, dc, 0), device_id_type=MESH)
    for dz, dc in zc:
        if dz != 0:
            pl.semaphore_signal(
                barrier, inc=1, device_id=at(0, 0, dc, dz), device_id_type=MESH
            )

    own_rows = pl.ds(pl.multiple_of(c * rows, rows), rows)
    sib_rows = pl.ds(pl.multiple_of(other * rows, rows), rows)

    def to_rows(dst, vec):
        for i in range(dst.shape[0]):
            dst[i : i + 1, :] = vec[:, i * LANES : (i + 1) * LANES]

    def spread(compact):
        for i in range(compact.shape[0]):
            rcol[i * LANES : (i + 1) * LANES, :] = jnp.broadcast_to(
                compact[i : i + 1, :], (LANES, LANES)
            ).T

    def contract(compact, mat, dst):
        count = compact.shape[0]
        high = compact.astype(BF16).astype(F32)
        low = compact - high
        terms = [
            jnp.concatenate([term[i : i + 1, :] for i in range(count)], 1)
            for term in (high, low)
        ]
        terms.append(jnp.zeros((14, count * LANES), F32))
        lhs = jnp.concatenate(terms, 0).astype(BF16)
        got = jnp.dot(lhs, mat[...], preferred_element_type=F32)
        to_rows(dst, got[0:1, :] + got[1:2, :])

    def exchange_start(own, msg, slots, ssem, rsem, targets):
        msg[...] = own[...].astype(BF16)
        for slot, target in targets:
            remote(msg, slots.at[slot], ssem, rsem, target).start()

    def exchange_sum(own, slots, rsem, count):
        settle(slots.at[pl.ds(1, count - 1)], rsem)
        total = own[...]
        for i in range(1, count):
            total = total + slots[i].astype(F32)
        return total

    targets_c = [(dy * nx + dx, at(dy, dx, 0, 0)) for dy, dx in xy]
    targets_r = [(dz * 2 + dc, at(0, 0, dc, dz)) for dz, dc in zc]

    loads[0].wait()
    uall[own_rows, :] = unit_norm(xs[...])
    for which in (1, 0):
        loads[2 - which].wait()
        cn[which] = unit_norm(cs[which].reshape(half, width))
        block = affinity(uall[own_rows, :], cn[which])
        if which == 1:
            ko[...] = block.astype(BF16)
        else:
            km[own_rows, :] = block.astype(BF16)
        to_rows(sums, jnp.sum(block, 0, keepdims=True))
        msg_0[which] = sums[...].astype(BF16)
    pl.semaphore_wait(barrier, len(xyc) + 2 * (nz - 1))
    for dy, dx, dc in xyc:
        remote(
            msg_0.at[dc], slots_0.at[(dy * nx + dx) * 2 + dc], sem_0.at[0], sem_0.at[1],
            at(dy, dx, dc, 0),
        ).start()
    send_rows = remote(
        uall.at[own_rows], uall.at[own_rows], sib_s.at[0], sib_r.at[0], sibling
    )
    send_rows.start()
    kt[:, own_rows] = affinity(cn[0], uall[own_rows, :]).astype(BF16)
    send_rows.wait()
    kt[:, sib_rows] = affinity(cn[0], uall[sib_rows, :]).astype(BF16)

    send_lists = None
    row_scale = None
    for it in range(ITERS):
        if it == 0:
            column_total = exchange_sum(sums, slots_0, sem_0.at[1], 2 * chips)
        else:
            own, slots = own_c.at[it - 1], slots_c.at[it - 1]
            contract(row_scale, km, own)
            exchange_start(
                own, msg_c.at[it - 1], slots, ssem_c.at[it - 1], rsem_c.at[it - 1], targets_c
            )
            column_total = exchange_sum(own, slots, rsem_c.at[it - 1], chips)
        list_scale = 1.0 / (total_lists * column_total)
        if it == ITERS - 1:
            list_own[...] = list_scale
            send_lists = remote(list_own, list_in, sib_s.at[1], sib_r.at[1], sibling)
            send_lists.start()
        contract(list_scale, kt, own_r.at[it])
        exchange_start(
            own_r.at[it], msg_r.at[it], slots_r.at[it], ssem_r.at[it], rsem_r.at[it], targets_r
        )
        if it == 0:
            km[sib_rows, :] = affinity(uall[sib_rows, :], cn[0]).astype(BF16)
            ut[...] = uall[...].astype(F32).T
        row_total = exchange_sum(own_r.at[it], slots_r.at[it], rsem_r.at[it], 2 * nz)
        row_scale = 1.0 / (total_rows * row_total)

    index = lax.broadcasted_iota(jnp.int32, (16, LANES), 0)
    for i in range(chip_rows // LANES):
        lanes = pl.ds(i * LANES, LANES)
        one = row_scale[i : i + 1, :]
        lhs_w[0:width, lanes] = (ut[:, lanes] * one).astype(BF16)
        high = one.astype(BF16).astype(F32)
        lhs_w[width : width + 16, lanes] = jnp.where(
            index == 0, high, jnp.where(index == 1, one - high, 0.0)
        ).astype(BF16)

    def reach(o):
        a, b = hops(o[0], ny), hops(o[1], nx)
        return (a * b == 0, -(4 * max(a, b) + a + b))

    order = sorted(xy + [(0, 0)], key=reach)
    cuts = [0] + list(range(2, chips, 4)) + [chips]
    for low, high in zip(cuts[:-1], cuts[1:]):
        group = order[low:high]
        blocks = []
        for dy, dx in group:
            dest = ((y + dy) % ny) * nx + (x + dx) % nx
            blocks.append(km[:, pl.ds(pl.multiple_of(dest * LANES, LANES), LANES)])
        got = jnp.dot(
            lhs_w[...], jnp.concatenate(blocks, 1), preferred_element_type=F32
        )
        for n, (dy, dx) in enumerate(group):
            slot = dy * nx + dx
            piece = got[:, n * LANES : (n + 1) * LANES]
            first = wa1.at[dy, 0] if dx == 0 else w_out.at[slot, pl.ds(0, part)]
            second = wb1.at[dx, 0] if dy == 0 else w_out.at[slot, pl.ds(part, part)]
            first[...] = piece[0:part].astype(BF16)
            second[...] = piece[part:width].astype(BF16)
            if dx != 0:
                remote(first, wa1.at[dy, dx], ss_a1.at[dy], rs_a1.at[dy], at(0, dx, 0, 0)).start()
            if dy != 0:
                remote(second, wb1.at[dx, dy], ss_b1.at[dx], rs_b1.at[dx], at(dy, 0, 0, 0)).start()
            mass = mass_in if slot == 0 else mass_out
            mass[slot] = piece[width : width + 1] + piece[width + 1 : width + 2]
            if slot != 0:
                remote(
                    mass_out.at[slot], mass_in.at[slot], sem_m.at[0], sem_m.at[1],
                    at(dy, dx, 0, 0),
                ).start()

    def assign():
        spread(total_rows * row_scale)
        send_lists.wait()
        for parity in range(2):
            @pl.when(c == parity)
            def _():
                def step(i, _):
                    here = pl.ds(pl.multiple_of(i * 16, 16), 16)
                    there = pl.ds(pl.multiple_of(parity * rows + i * 16, 16), 16)
                    scale = rcol[there, :]
                    for j in range(half // LANES):
                        lanes = pl.ds(j * LANES, LANES)
                        one = km[there, lanes].astype(F32) * scale * list_own[j : j + 1, :]
                        two = ko[here, lanes].astype(F32) * scale * list_in[j : j + 1, :]
                        out[here, pl.ds((2 * j + parity) * LANES, LANES)] = one.astype(BF16)
                        out[here, pl.ds((2 * j + 1 - parity) * LANES, LANES)] = two.astype(BF16)
                    return 0

                lax.fori_loop(0, rows // 16, step, 0)

    def gather(slots, count):
        total = slots[0].astype(F32)
        for i in range(1, count):
            total = total + slots[i].astype(F32)
        return total

    def stage_a(dy):
        settle(wa1.at[dy, pl.ds(1, nx - 1)], rs_a1.at[dy])
        return gather(wa1.at[dy], nx)

    def stage_b(dx):
        settle(wb1.at[dx, pl.ds(1, ny - 1)], rs_b1.at[dx])
        return gather(wb1.at[dx], ny)

    for step in sorted(range(1, ny), key=lambda o: -hops(o, ny)):
        wa2_out[step] = stage_a(step).astype(BF16)
        remote(wa2_out.at[step], wa2.at[step], ss_2.at[0], rs_2.at[0], at(step, 0, 0, 0)).start()
        wb2_out[step] = stage_b(step).astype(BF16)
        remote(wb2_out.at[step], wb2.at[step], ss_2.at[1], rs_2.at[1], at(0, step, 0, 0)).start()

    assign()

    first = stage_a(0)
    second = stage_b(0)
    settle(mass_in.at[pl.ds(1, chips - 1)], sem_m.at[1])
    mass = mass_in[0]
    for i in range(1, chips):
        mass = mass + mass_in[i]
    raw[width : width + 8, :] = jnp.broadcast_to(mass, (8, LANES))
    settle(wa2.at[pl.ds(1, ny - 1)], rs_2.at[0])
    for i in range(1, ny):
        first = first + wa2[i].astype(F32)
    raw[0:part, :] = first
    settle(wb2.at[pl.ds(1, nx - 1)], rs_2.at[1])
    for i in range(1, nx):
        second = second + wb2[i].astype(F32)
    raw[part:width, :] = second

    for i in range(ny):
        settle(wa1.at[i, pl.ds(1, nx - 1)], ss_a1.at[i])
    for i in range(nx):
        settle(wb1.at[i, pl.ds(1, ny - 1)], ss_b1.at[i])
    settle(wa2.at[pl.ds(1, ny - 1)], ss_2.at[0])
    settle(wb2.at[pl.ds(1, nx - 1)], ss_2.at[1])
    settle(mass_in.at[pl.ds(1, chips - 1)], sem_m.at[0])
    settle(slots_0.at[pl.ds(1, 2 * chips - 1)], sem_0.at[0])
    for it in range(ITERS - 1):
        settle(slots_c.at[it, pl.ds(1, chips - 1)], ssem_c.at[it])
    for it in range(ITERS):
        settle(slots_r.at[it, pl.ds(1, 2 * nz - 1)], ssem_r.at[it])


def write_out(assignment, raw, out, out_centers, centers, sems):
    pieces = 8
    size = assignment.shape[0] // pieces
    copies = [
        pltpu.make_async_copy(
            assignment.at[pl.ds(i * size, size)], out.at[pl.ds(i * size, size)], sems.at[i]
        )
        for i in range(pieces)
    ]
    for copy in copies:
        copy.start()
    width = centers.shape[1]
    scale = jnp.sqrt(F32(width)) / raw[width : width + 1, :]
    centers[...] = (raw[0:width, :] * scale).T
    copies.append(pltpu.make_async_copy(centers, out_centers, sems.at[pieces]))
    copies[-1].start()
    for copy in copies:
        copy.wait()


def solution(mesh):
    row_devices = mesh.shape["rows"]
    nz = mesh.shape["lists"]
    ny = nx = round((row_devices // 2) ** 0.5)

    def body(samples, centers):
        rows, width = samples.shape
        lists = centers.shape[0]
        half, chip_rows, chips = lists // 2, 2 * rows, ny * nx
        mc, mr = half // LANES, chip_rows // LANES
        part = width // 2
        dma = pltpu.SemaphoreType.DMA
        vmem = pl.BlockSpec(memory_space=pltpu.VMEM)
        hbm = pl.BlockSpec(memory_space=pl.ANY)
        big = ((rows, lists), BF16)
        small = ((lists // row_devices, width), F32)
        sums = ((width + 8, LANES), F32)
        assignment, raw = pl.pallas_call(
            functools.partial(
                kernel, ny, nx, nz, float(rows * row_devices), float(lists * nz)
            ),
            out_shape=(pltpu.VMEM(*big), pltpu.VMEM(*sums)),
            in_specs=[hbm, hbm],
            out_specs=(vmem, vmem),
            scratch_shapes=[
                pltpu.VMEM((rows, width), BF16),
                pltpu.VMEM((2, half // LANES, LANES, width), BF16),
                pltpu.VMEM((chip_rows, width), BF16),
                pltpu.VMEM((2, half, width), BF16),
                pltpu.VMEM((chip_rows, half), BF16),
                pltpu.VMEM((rows, half), BF16),
                pltpu.VMEM((half, chip_rows), BF16),
                pltpu.VMEM((width, chip_rows), F32),
                pltpu.VMEM((width + 16, chip_rows), BF16),
                pltpu.VMEM((max(half, chip_rows), LANES), F32),
                pltpu.VMEM((mc, LANES), F32),
                pltpu.VMEM((2, mc, LANES), BF16),
                pltpu.VMEM((2 * chips, mc, LANES), BF16),
                pltpu.VMEM((ITERS - 1, mc, LANES), F32),
                pltpu.VMEM((ITERS - 1, mc, LANES), BF16),
                pltpu.VMEM((ITERS - 1, chips, mc, LANES), BF16),
                pltpu.VMEM((ITERS, mr, LANES), F32),
                pltpu.VMEM((ITERS, mr, LANES), BF16),
                pltpu.VMEM((ITERS, 2 * nz, mr, LANES), BF16),
                pltpu.VMEM((mc, LANES), F32),
                pltpu.VMEM((mc, LANES), F32),
                pltpu.VMEM((chips, 1, LANES), F32),
                pltpu.VMEM((chips, 1, LANES), F32),
                pltpu.VMEM((chips, width, LANES), BF16),
                pltpu.VMEM((ny, nx, part, LANES), BF16),
                pltpu.VMEM((nx, ny, part, LANES), BF16),
                pltpu.VMEM((ny, part, LANES), BF16),
                pltpu.VMEM((nx, part, LANES), BF16),
                pltpu.VMEM((ny, part, LANES), BF16),
                pltpu.VMEM((nx, part, LANES), BF16),
                dma((3,)),
                dma((2,)),
                dma((ITERS - 1,)),
                dma((ITERS - 1,)),
                dma((ITERS,)),
                dma((ITERS,)),
                dma((2,)),
                dma((2,)),
                dma((2,)),
                dma((ny,)),
                dma((ny,)),
                dma((nx,)),
                dma((nx,)),
                dma((2,)),
                dma((2,)),
            ],
            compiler_params=pltpu.CompilerParams(
                collective_id=0, has_side_effects=True, vmem_limit_bytes=50 * 2**20
            ),
        )(samples, centers.reshape(half // LANES, 2, LANES, width))
        return tuple(
            pl.pallas_call(
                write_out,
                out_shape=(jax.ShapeDtypeStruct(*big), jax.ShapeDtypeStruct(*small)),
                in_specs=[vmem, vmem],
                out_specs=(hbm, hbm),
                scratch_shapes=[pltpu.VMEM(*small), dma((9,))],
                compiler_params=pltpu.CompilerParams(vmem_limit_bytes=2**20),
            )(
                pltpu.with_memory_space_constraint(assignment, pltpu.VMEM),
                pltpu.with_memory_space_constraint(raw, pltpu.VMEM),
            )
        )

    return jax.shard_map(
        body,
        mesh=mesh,
        in_specs=(P("rows", None), P("lists", None)),
        out_specs=(P("rows", "lists"), P(("lists", "rows"), None)),
        check_vma=False,
    )
```

time: 66 us -> 61.6 us (0.933)
  Pallas kernels: 65.1 us -> 60.6 us
    pallas_call x1, Pallas kernels: 61.8 us -> 57.3 us  [body(): pl.pallas_call(functools.partial(kernel, ny, nx, nz, float(rows * row_dev...]
where the time goes in v3:
time: 61.6 us; the launch traced here: 61.4 us
  Pallas kernels  60.6 us (98%)
  between operations  0.8 us (1%)
    pallas_call x1, Pallas kernels, body(): pl.pallas_call(functools.partial(kernel, ny, nx, nz, float(rows * row_dev...  57.3 us
    pallas_call x1, Pallas kernels, body(): pl.pallas_call(write_out, out_shape=(jax.ShapeDtypeStruct(*big), jax.Shap...  3.38 us

profile of v3, /device:TPU:1, one launch (start us, length us, event | category | flops | bytes accessed | tf_op | source)
XLA Modules:
  0.0 61.4 jit_solution(8181833720679735469)
XLA Ops:
  0.6 57.3 %shard_map.41 = (bf16[1024,4096]{1,0:T(8,128)(2,1)S(1)}, f32[264,128]{1,0:T(8,128)S(1)}) custom-call(bf16[1024,256]{1,0:T(8,128)(2,1)} %samples.1, bf16[16,2,128,256]{3,2,1,0:T(8,128)(2,1)} %bitcast.1), custom_call_target="tpu_custom_call" | custom-call | tf_op jit(solution)/shard_map/pallas_call | solution.py:342
  57.9 3.4 %shard_map.42 = (bf16[1024,4096]{1,0:T(8,128)(2,1)}, f32[128,256]{1,0:T(8,128)}) custom-call(bf16[1024,4096]{1,0:T(8,128)(2,1)S(1)} %get-tuple-element.4.assignment, f32[264,128]{1,0:T(8,128)S(1)} %get-tuple-element.5.raw), custom_call_target="tpu_custom_call" | custom-call | tf_op jit(solution)/shard_map/pallas_call | solution.py:401

commit v4 on v3

--- a/solution.py
+++ b/solution.py
@@ -37,8 +37,8 @@
     xs, cs, uall, cn, km, ko, kt, ut, lhs_w, rcol, sums,
     msg_0, slots_0, own_c, msg_c, slots_c, own_r, msg_r, slots_r, list_own, list_in,
     mass_out, mass_in, w_out, wa1, wb1, wa2_out, wb2_out, wa2, wb2,
-    in_sem, sem_0, ssem_c, rsem_c, ssem_r, rsem_r, sib_s, sib_r, sem_m,
-    ss_a1, rs_a1, ss_b1, rs_b1, ss_2, rs_2,
+    ra, rb, ma, mb, in_sem, sem_0, ssem_c, rsem_c, ssem_r, rsem_r, sib_s, sib_r, sem_m,
+    ss_a1, rs_a1, ss_b1, rs_b1, ss_2, rs_2, ss_f, rs_fa, rs_fb,
 ):
     rows, width = xs.shape
     half = cs.shape[1] * LANES
@@ -196,12 +196,44 @@
             index == 0, high, jnp.where(index == 1, one - high, 0.0)
         ).astype(BF16)
 
+    merged = nx == 4
+    hp = part // 2
+
     def reach(o):
         a, b = hops(o[0], ny), hops(o[1], nx)
-        return (a * b == 0, -(4 * max(a, b) + a + b))
+        return -(4 * max(a, b) + a + b)
+
+    def first_stage(piece, d, step_to, line, far, ssem, rsem, far_ssem, far_rsem):
+        top, bottom = piece.at[pl.ds(0, hp)], piece.at[pl.ds(hp, hp)]
+        if not merged:
+            remote(piece, line.at[d], ssem, rsem, step_to(d)).start()
+        elif d == 2:
+            remote(top, far.at[0], far_ssem, far_rsem, step_to(1)).start()
+            remote(bottom, far.at[1], far_ssem, far_rsem, step_to(3)).start()
+        elif d == 1:
+            remote(bottom, line.at[1, pl.ds(hp, hp)], ssem, rsem, step_to(1)).start()
+        else:
+            remote(top, line.at[2, pl.ds(0, hp)], ssem, rsem, step_to(3)).start()
+
+    def merge(right, left, step_to, line, far, out_pieces, ssem, rsem, far_rsem):
+        settle(far, far_rsem)
+        out_pieces[0] = (right.astype(F32) + far[0].astype(F32)).astype(BF16)
+        remote(
+            out_pieces.at[0], line.at[1, pl.ds(0, hp)], ssem, rsem, step_to(1)
+        ).start()
+        out_pieces[1] = (left.astype(F32) + far[1].astype(F32)).astype(BF16)
+        remote(
+            out_pieces.at[1], line.at[2, pl.ds(hp, hp)], ssem, rsem, step_to(3)
+        ).start()
+
+    def along_x(d):
+        return at(0, d, 0, 0)
+
+    def along_y(d):
+        return at(d, 0, 0, 0)
 
     order = sorted(xy + [(0, 0)], key=reach)
-    cuts = [0] + list(range(2, chips, 4)) + [chips]
+    cuts = list(range(0, chips + 1, 4))
     for low, high in zip(cuts[:-1], cuts[1:]):
         group = order[low:high]
         blocks = []
@@ -219,9 +251,15 @@
             first[...] = piece[0:part].astype(BF16)
             second[...] = piece[part:width].astype(BF16)
             if dx != 0:
-                remote(first, wa1.at[dy, dx], ss_a1.at[dy], rs_a1.at[dy], at(0, dx, 0, 0)).start()
+                first_stage(
+                    first, dx, along_x, wa1.at[dy], ra.at[dy], ss_a1.at[dy], rs_a1.at[dy],
+                    ss_f.at[0], rs_fa.at[dy],
+                )
             if dy != 0:
-                remote(second, wb1.at[dx, dy], ss_b1.at[dx], rs_b1.at[dx], at(dy, 0, 0, 0)).start()
+                first_stage(
+                    second, dy, along_y, wb1.at[dx], rb.at[dx], ss_b1.at[dx], rs_b1.at[dx],
+                    ss_f.at[1], rs_fb.at[dx],
+                )
             mass = mass_in if slot == 0 else mass_out
             mass[slot] = piece[width : width + 1] + piece[width + 1 : width + 2]
             if slot != 0:
@@ -230,9 +268,7 @@
                     at(dy, dx, 0, 0),
                 ).start()
 
-    def assign():
-        spread(total_rows * row_scale)
-        send_lists.wait()
+    def assign(start, stop):
         for parity in range(2):
             @pl.when(c == parity)
             def _():
@@ -248,21 +284,38 @@
                         out[here, pl.ds((2 * j + 1 - parity) * LANES, LANES)] = two.astype(BF16)
                     return 0
 
-                lax.fori_loop(0, rows // 16, step, 0)
-
-    def gather(slots, count):
+                lax.fori_loop(start, stop, step, 0)
+
+    steps = rows // 16
+    if merged:
+        for d in sorted(range(nx), key=lambda o: -hops(o, nx) if o else 0):
+            merge(
+                w_out[d * nx + 1, 0:hp, :], w_out[d * nx + 3, hp:part, :], along_x,
+                wa1.at[d], ra.at[d], ma.at[d], ss_a1.at[d], rs_a1.at[d], rs_fa.at[d],
+            )
+            merge(
+                w_out[nx + d, part : part + hp, :], w_out[3 * nx + d, part + hp : width, :],
+                along_y, wb1.at[d], rb.at[d], mb.at[d], ss_b1.at[d], rs_b1.at[d], rs_fb.at[d],
+            )
+    spread(total_rows * row_scale)
+    send_lists.wait()
+    assign(0, steps // 2)
+    line_count = 2 if merged else nx - 1
+    line_slots = pl.ds(1, line_count)
+
+    def gather(slots):
         total = slots[0].astype(F32)
-        for i in range(1, count):
+        for i in range(1, 1 + line_count):
             total = total + slots[i].astype(F32)
         return total
 
     def stage_a(dy):
-        settle(wa1.at[dy, pl.ds(1, nx - 1)], rs_a1.at[dy])
-        return gather(wa1.at[dy], nx)
+        settle(wa1.at[dy, line_slots], rs_a1.at[dy])
+        return gather(wa1.at[dy])
 
     def stage_b(dx):
-        settle(wb1.at[dx, pl.ds(1, ny - 1)], rs_b1.at[dx])
-        return gather(wb1.at[dx], ny)
+        settle(wb1.at[dx, line_slots], rs_b1.at[dx])
+        return gather(wb1.at[dx])
 
     for step in sorted(range(1, ny), key=lambda o: -hops(o, ny)):
         wa2_out[step] = stage_a(step).astype(BF16)
@@ -270,7 +323,7 @@
         wb2_out[step] = stage_b(step).astype(BF16)
         remote(wb2_out.at[step], wb2.at[step], ss_2.at[1], rs_2.at[1], at(0, step, 0, 0)).start()
 
-    assign()
+    assign(steps // 2, steps)
 
     first = stage_a(0)
     second = stage_b(0)
@@ -289,11 +342,14 @@
     raw[part:width, :] = second
 
     for i in range(ny):
-        settle(wa1.at[i, pl.ds(1, nx - 1)], ss_a1.at[i])
+        settle(wa1.at[i, line_slots], ss_a1.at[i])
     for i in range(nx):
-        settle(wb1.at[i, pl.ds(1, ny - 1)], ss_b1.at[i])
+        settle(wb1.at[i, line_slots], ss_b1.at[i])
     settle(wa2.at[pl.ds(1, ny - 1)], ss_2.at[0])
     settle(wb2.at[pl.ds(1, nx - 1)], ss_2.at[1])
+    if merged:
+        settle(ra, ss_f.at[0])
+        settle(rb, ss_f.at[1])
     settle(mass_in.at[pl.ds(1, chips - 1)], sem_m.at[0])
     settle(slots_0.at[pl.ds(1, 2 * chips - 1)], sem_0.at[0])
     for it in range(ITERS - 1):
@@ -371,12 +427,16 @@
                 pltpu.VMEM((chips, 1, LANES), F32),
                 pltpu.VMEM((chips, 1, LANES), F32),
                 pltpu.VMEM((chips, width, LANES), BF16),
-                pltpu.VMEM((ny, nx, part, LANES), BF16),
-                pltpu.VMEM((nx, ny, part, LANES), BF16),
+                pltpu.VMEM((ny, 3, part, LANES), BF16),
+                pltpu.VMEM((nx, 3, part, LANES), BF16),
                 pltpu.VMEM((ny, part, LANES), BF16),
                 pltpu.VMEM((nx, part, LANES), BF16),
                 pltpu.VMEM((ny, part, LANES), BF16),
                 pltpu.VMEM((nx, part, LANES), BF16),
+                pltpu.VMEM((ny, 2, part // 2, LANES), BF16),
+                pltpu.VMEM((nx, 2, part // 2, LANES), BF16),
+                pltpu.VMEM((ny, 2, part // 2, LANES), BF16),
+                pltpu.VMEM((nx, 2, part // 2, LANES), BF16),
                 dma((3,)),
                 dma((2,)),
                 dma((ITERS - 1,)),
@@ -392,6 +452,9 @@
                 dma((nx,)),
                 dma((2,)),
                 dma((2,)),
+                dma((2,)),
+                dma((ny,)),
+                dma((nx,)),
             ],
             compiler_params=pltpu.CompilerParams(
                 collective_id=0, has_side_effects=True, vmem_limit_bytes=50 * 2**20

time: 61.6 us -> 61.1 us (level)
  Pallas kernels: 60.6 us -> 59.9 us
    pallas_call x1, Pallas kernels: 57.3 us -> 56.6 us  [body(): pl.pallas_call(functools.partial(kernel, ny, nx, nz, float(rows * row_dev...]
where the time goes in v4:
time: 61.1 us; the launch traced here: 60.7 us
  Pallas kernels  59.9 us (98%)
  between operations  0.8 us (1%)
    pallas_call x1, Pallas kernels, body(): pl.pallas_call(functools.partial(kernel, ny, nx, nz, float(rows * row_dev...  56.6 us
    pallas_call x1, Pallas kernels, body(): pl.pallas_call(write_out, out_shape=(jax.ShapeDtypeStruct(*big), jax.Shap...  3.38 us

profile of v4, /device:TPU:1, one launch (start us, length us, event | category | flops | bytes accessed | tf_op | source)
XLA Modules:
  0.0 60.7 jit_solution(11925746280152112826)
XLA Ops:
  0.6 56.6 %shard_map.41 = (bf16[1024,4096]{1,0:T(8,128)(2,1)S(1)}, f32[264,128]{1,0:T(8,128)S(1)}) custom-call(bf16[1024,256]{1,0:T(8,128)(2,1)} %samples.1, bf16[16,2,128,256]{3,2,1,0:T(8,128)(2,1)} %bitcast.1), custom_call_target="tpu_custom_call" | custom-call | tf_op jit(solution)/shard_map/pallas_call | solution.py:398
  57.2 3.4 %shard_map.42 = (bf16[1024,4096]{1,0:T(8,128)(2,1)}, f32[128,256]{1,0:T(8,128)}) custom-call(bf16[1024,4096]{1,0:T(8,128)(2,1)S(1)} %get-tuple-element.4.assignment, f32[264,128]{1,0:T(8,128)S(1)} %get-tuple-element.5.raw), custom_call_target="tpu_custom_call" | custom-call | tf_op jit(solution)/shard_map/pallas_call | solution.py:464

commit v5 on v4

--- a/solution.py
+++ b/solution.py
@@ -325,6 +325,20 @@
 
     assign(steps // 2, steps)
 
+    for i in range(ny):
+        settle(wa1.at[i, line_slots], ss_a1.at[i])
+    for i in range(nx):
+        settle(wb1.at[i, line_slots], ss_b1.at[i])
+    if merged:
+        settle(ra, ss_f.at[0])
+        settle(rb, ss_f.at[1])
+    settle(mass_in.at[pl.ds(1, chips - 1)], sem_m.at[0])
+    settle(slots_0.at[pl.ds(1, 2 * chips - 1)], sem_0.at[0])
+    for it in range(ITERS - 1):
+        settle(slots_c.at[it, pl.ds(1, chips - 1)], ssem_c.at[it])
+    for it in range(ITERS):
+        settle(slots_r.at[it, pl.ds(1, 2 * nz - 1)], ssem_r.at[it])
+
     first = stage_a(0)
     second = stage_b(0)
     settle(mass_in.at[pl.ds(1, chips - 1)], sem_m.at[1])
@@ -340,22 +354,8 @@
     for i in range(1, nx):
         second = second + wb2[i].astype(F32)
     raw[part:width, :] = second
-
-    for i in range(ny):
-        settle(wa1.at[i, line_slots], ss_a1.at[i])
-    for i in range(nx):
-        settle(wb1.at[i, line_slots], ss_b1.at[i])
     settle(wa2.at[pl.ds(1, ny - 1)], ss_2.at[0])
     settle(wb2.at[pl.ds(1, nx - 1)], ss_2.at[1])
-    if merged:
-        settle(ra, ss_f.at[0])
-        settle(rb, ss_f.at[1])
-    settle(mass_in.at[pl.ds(1, chips - 1)], sem_m.at[0])
-    settle(slots_0.at[pl.ds(1, 2 * chips - 1)], sem_0.at[0])
-    for it in range(ITERS - 1):
-        settle(slots_c.at[it, pl.ds(1, chips - 1)], ssem_c.at[it])
-    for it in range(ITERS):
-        settle(slots_r.at[it, pl.ds(1, 2 * nz - 1)], ssem_r.at[it])
 
 
 def write_out(assignment, raw, out, out_centers, centers, sems):

time: 61.1 us -> 61.1 us (level)
  no operation moved by 1% of the time
where the time goes in v5:
time: 61.1 us; the launch traced here: 60.7 us
  Pallas kernels  59.9 us (98%)
  between operations  0.8 us (1%)
    pallas_call x1, Pallas kernels, body(): pl.pallas_call(functools.partial(kernel, ny, nx, nz, float(rows * row_dev...  56.5 us
    pallas_call x1, Pallas kernels, body(): pl.pallas_call(write_out, out_shape=(jax.ShapeDtypeStruct(*big), jax.Shap...  3.38 us

profile of v5, /device:TPU:1, one launch (start us, length us, event | category | flops | bytes accessed | tf_op | source)
XLA Modules:
  0.0 60.7 jit_solution(9153535733032293571)
XLA Ops:
  0.6 56.5 %shard_map.41 = (bf16[1024,4096]{1,0:T(8,128)(2,1)S(1)}, f32[264,128]{1,0:T(8,128)S(1)}) custom-call(bf16[1024,256]{1,0:T(8,128)(2,1)} %samples.1, bf16[16,2,128,256]{3,2,1,0:T(8,128)(2,1)} %bitcast.1), custom_call_target="tpu_custom_call" | custom-call | tf_op jit(solution)/shard_map/pallas_call | solution.py:398
  57.2 3.4 %shard_map.42 = (bf16[1024,4096]{1,0:T(8,128)(2,1)}, f32[128,256]{1,0:T(8,128)}) custom-call(bf16[1024,4096]{1,0:T(8,128)(2,1)S(1)} %get-tuple-element.4.assignment, f32[264,128]{1,0:T(8,128)S(1)} %get-tuple-element.5.raw), custom_call_target="tpu_custom_call" | custom-call | tf_op jit(solution)/shard_map/pallas_call | solution.py:464
